TPU v7x, 512 devices: a whole 4x4x16 slice. The times are simulated.
512 devices in a mesh: dp: 32 (over z, core), vocab: 16 (over y, x).
Axes of the slice: x: 4, y: 4, z: 16, core: 2. Of those that a mesh axis runs over, the one named last changes fastest.
Arguments:
- hidden: bfloat16 [640, 12288], P(None, 'dp'), may hold values from -4 to 4
- table: bfloat16 [32768, 12288], P('vocab', 'dp'), may hold values from -1.2 to 1.2
- targets: int32 [640], replicated, may hold values from 0 to 32767
- owners: int32 [640, 1], replicated, may hold values from 0 to 15; in each aligned block of 40 rows (0 to 39, 40 to 79, ...) at most 10 rows name the same one
- rows: int32 [640], replicated, may hold values from 0 to 2047
- input_grad: bfloat16 [640, 12288], P('vocab', 'dp'), may hold values from -6 to 6
Outputs:
- token_loss: float32 [640], P('dp')
- hidden_grad: bfloat16 [640, 12288], P('vocab', 'dp')
- table_grad: float32 [32768, 12288], P('vocab', 'dp')
Inputs may be any that keep to these rules, and one draw needn't show every extreme that they name: `owners`: in each aligned block of 40 tokens, no owner is named more than 10 times, a bound that some block reaches.
All inputs are finite; a program needn't handle non-finite values.
Results may differ from a plain program's by a relative error of at most 0.0034.
Values may be sent and summed in bfloat16 or wider, within the bound.
A program may use at most 64 MiB of HBM per device.

v0:
```python
import jax
import jax.numpy as jnp
from jax import lax
from jax.sharding import PartitionSpec as P

logit_scale = 0.8333333


def combine_stats(logits, local_max, local_target):
    largest = lax.pmax(local_max, "vocab")
    local_exp = jnp.sum(jnp.exp(logits - largest[:, None]), axis=1)
    totals = lax.psum((local_exp, local_target), "vocab")
    return (largest, totals[0], totals[1])


def on_device(hidden, table, targets, owners, rows, input_grad):
    dp_count = lax.axis_size("dp")
    vocab_count = lax.axis_size("vocab")
    token_count = hidden.shape[0]
    width_part = hidden.shape[1]
    vocab_part = table.shape[0]
    block_rows = token_count // dp_count
    token_block = token_count // vocab_count
    vocab_index = lax.axis_index("vocab")
    columns = vocab_index * vocab_part + jnp.arange(vocab_part, dtype=jnp.int32)
    picked = hidden
    logits = logit_scale * lax.psum(
        lax.dot_general(
            picked, table, (((1,), (1,)), ((), ())), preferred_element_type=jnp.float32
        ),
        "dp",
    )
    aimed = targets[:, None] == columns[None, :]
    local_max = jnp.max(logits, axis=1)
    local_target = jnp.sum(jnp.where(aimed, logits, 0.0), axis=1)
    total_max, total_exp, total_target = combine_stats(logits, local_max, local_target)
    log_total = total_max + jnp.log(total_exp)
    loss_rows = log_total - total_target
    grads = (jnp.exp(logits - log_total[:, None]) - aimed.astype(jnp.float32)).astype(jnp.bfloat16)
    token_loss = lax.dynamic_slice_in_dim(
        loss_rows, lax.axis_index("dp") * block_rows, block_rows, 0
    )
    picked = grads
    hidden_sum = lax.psum_scatter(
        jnp.dot(picked, table, preferred_element_type=jnp.float32),
        "vocab",
        scatter_dimension=0,
        tiled=True,
    )
    head_grad = lax.dot_general(
        grads, hidden, (((0,), (0,)), ((), ())), preferred_element_type=jnp.float32
    )
    hidden_grad = (logit_scale * hidden_sum).astype(jnp.bfloat16)
    owner_list = owners[:, 0]
    mine = owner_list == vocab_index
    vocab_iota = jnp.arange(vocab_part, dtype=jnp.int32)
    capacity = 4 * token_count // (vocab_count * vocab_count)
    slot_total = vocab_count * capacity
    owner_hits = (owner_list[:, None] == jnp.arange(vocab_count, dtype=jnp.int32)[None, :]).astype(
        jnp.int32
    )
    running = jnp.cumsum(owner_hits.reshape(vocab_count, token_block, vocab_count), axis=1).reshape(
        token_count, vocab_count
    )
    ranks = jnp.sum(owner_hits * running, axis=1) - 1
    own_start = vocab_index * token_block
    send_slots = lax.dynamic_slice_in_dim(owner_list * capacity + ranks, own_start, token_block, 0)
    slot_iota = jnp.arange(slot_total, dtype=jnp.int32)
    packer = (slot_iota[:, None] == send_slots[None, :]).astype(jnp.bfloat16)
    outgoing = jnp.dot(packer, input_grad, preferred_element_type=jnp.float32).astype(jnp.bfloat16)
    incoming = lax.all_to_all(
        outgoing.reshape(vocab_count, capacity, width_part),
        "vocab",
        split_axis=0,
        concat_axis=0,
        tiled=True,
    )
    source_block = jnp.arange(token_count, dtype=jnp.int32) // token_block
    arrive_slots = source_block * capacity + ranks
    placed = ((arrive_slots[:, None] == slot_iota[None, :]) & mine[:, None]).astype(jnp.bfloat16)
    landing = (rows[:, None] == vocab_iota[None, :]).astype(jnp.bfloat16)
    slot_rows = lax.dot_general(
        placed, landing, (((0,), (0,)), ((), ())), preferred_element_type=jnp.float32
    ).astype(jnp.bfloat16)
    embed_grad = lax.dot_general(
        slot_rows,
        incoming.reshape(slot_total, width_part),
        (((0,), (0,)), ((), ())),
        preferred_element_type=jnp.float32,
    )
    table_grad = logit_scale * head_grad + embed_grad
    return (token_loss, hidden_grad, table_grad)


def solution(mesh):
    return jax.shard_map(
        on_device,
        mesh=mesh,
        in_specs=(P(None, "dp"), P("vocab", "dp"), P(), P(), P(), P("vocab", "dp")),
        out_specs=(P("dp"), P("vocab", "dp"), P("vocab", "dp")),
        check_vma=False,
    )
```

profile of v0, /device:TPU:1, one launch (start us, length us, event | category | flops | bytes accessed | tf_op | source)
XLA Modules:
  0.0 454.0 jit_solution(2658075158801071667)
XLA Ops:
  7.2 0.0 copy-start
  7.2 0.0 all-reduce.5.cloned.1.call-start
  7.2 1.4 copy-done
  8.6 4.9 %fusion.25 = f32[640,2048]{1,0:T(8,128)} fusion(bf16[640,384]{1,0:T(8,128)(2,1)} %param.6, bf16[2048,384]{1,0:T(8,128)(2,1)S(1)} %copy-done), kind=kOutput, calls=%fused_computation.42 | convolution fusion | flops 1006632960 | bytes 7307264 | tf_op jit(solution)/shard_map/dot_general | solution.py:28
  13.5 0.0 all-reduce.5.cloned.1.call-update
  13.5 0.0 all-reduce.7.cloned.1.call-start
  13.6 0.6 copy-done.5
  14.2 0.1 eq.79
  14.3 0.1 copy.14
  14.4 0.9 fusion.24
  15.3 0.1 copy.15
  15.4 0.1 sub.42
  15.5 0.1 dynamic_slice.7
  15.6 227.5 %all-reduce.5.cloned.1.call-done = f32[640,2048]{1,0:T(8,128)} async-done(((f32[640,2048]{1,0:T(8,128)}), f32[640,2048]{1,0:T(8,128)}) %all-reduce.5.cloned.1.call-update) | async-done | bytes 5242896 | tf_op jit(solution)/shard_map/psum | solution.py:27
  243.1 2.9 multiply_reduce_fusion
  246.0 33.1 %pmax.7 = f32[640]{0:T(1024)S(1)} all-reduce(f32[640]{0:T(1024)S(1)} %multiply_reduce_fusion), channel_id=1, replica_groups=mesh['dp'=32,'vocab'=16] {'vocab'}, use_global_device_ids=true, to_apply=%region_2.3 | all-reduce | flops 640 | bytes 5120 | tf_op jit(solution)/shard_map/pmax | solution.py:10
  279.1 4.1 fusion
  283.3 29.0 %all-reduce.1 = (f32[640]{0:T(1024)S(1)}, f32[640]{0:T(1024)S(1)}) all-reduce(f32[640]{0:T(1024)S(1)} %get-tuple-element.4, f32[640]{0:T(1024)S(1)} %get-tuple-element.3), channel_id=1, replica_groups=mesh['dp'=32,'vocab'=16] {'vocab'}, use_global_device_ids=true, to_apply=%region_4.5 | all-reduce | flops 1280 | bytes 10240 | tf_op jit(solution)/shard_map/psum | solution.py:12
  312.3 3.3 fusion.2
  315.6 1.5 copy-done.1
  317.1 2.5 fusion.26
  319.6 0.0 all-reduce.7.cloned.1.call-update
  319.6 0.2 convolution_convert_fusion
  319.8 0.7 reshape.65
  320.5 3.5 all-to-all-start
  324.1 1.3 dynamic-slice
  326.0 5.2 %all-to-all-done = bf16[16,10,384]{2,1,0:T(8,128)(2,1)S(1)} async-done(((bf16[16,10,384]{2,1,0:T(8,128)(2,1)}), bf16[16,10,384]{2,1,0:T(8,128)(2,1)S(1)}, u32[]{:S(2)}, u32[]{:S(2)}) %all-to-all-start) | async-done | bytes 122912 | tf_op jit(solution)/shard_map/all_to_all | solution.py:71
  331.3 0.6 dynamic_slice.6
  331.9 5.1 %fusion.27 = f32[2048,384]{1,0:T(8,128)} fusion(bf16[640,2048]{1,0:T(8,128)(2,1)} %copy-done.1, bf16[640,384]{1,0:T(8,128)(2,1)S(1)} %copy-done.2), kind=kOutput, calls=%fused_computation.44 | convolution fusion | flops 1006632960 | bytes 6258688 | tf_op jit(solution)/shard_map/dot_general | solution.py:50
  337.0 5.6 %multiply_add_fusion = f32[2048,384]{1,0:T(8,128)} fusion(f32[2048,384]{1,0:T(8,128)} %fusion.27, bf16[160,384]{1,0:T(8,128)(2,1)S(1)} %reshape.66, s32[640]{0:T(1024)S(1)} %copy-done.6, s32[640]{0:T(1024)S(1)} %get-tuple-element.11, pred[640]{0:T(1024)(128)(4,1)S(1)} %compare_reduce_fusion), kind=kOutput, calls=%fused_computation.9 | convolution fusion | flops 674504704 | bytes 6420096 | tf_op jit(solution)/shard_map/dot_general | solution.py:85
  342.6 103.2 %all-reduce.7.cloned.1.call-done = f32[640,384]{1,0:T(8,128)} async-done(((f32[640,384]{1,0:T(8,128)}), f32[640,384]{1,0:T(8,128)}) %all-reduce.7.cloned.1.call-update) | async-done | bytes 983056
  445.8 1.4 fusion.15
  (17 shorter events, 0.1 us)
Async XLA Ops:
  7.2 1.4 copy-start
  7.2 235.9 %all-reduce.5.cloned.1.call-start = ((), (), s32[]{:S(2)}) async-start(), calls=%async_computation.1 | async-start | bytes 10485760 | tf_op jit(solution)/shard_map/psum | solution.py:27
  13.5 0.7 copy-start.5
  13.5 265.6 %copy-start.4 = (s32[640]{0:T(1024)S(1)}, s32[640]{0:T(1024)}, u32[]{:S(2)}) copy-start(s32[640]{0:T(1024)} %param.8) | copy-start | bytes 7684
  13.5 432.2 %all-reduce.7.cloned.1.call-start = ((), (), s32[]{:S(2)}) async-start(), calls=%async_computation.2 | async-start | bytes 1966080
  315.6 1.5 copy-start.1
  317.1 2.5 copy-start.3
  317.1 14.7 %copy-start.2 = (bf16[640,384]{1,0:T(8,128)(2,1)S(1)}, bf16[640,384]{1,0:T(8,128)(2,1)}, u32[]{:S(2)}) copy-start(bf16[640,384]{1,0:T(8,128)(2,1)} %param.6) | copy-start | bytes 1474564
  319.6 17.4 %copy-start.6 = (s32[640]{0:T(1024)S(1)}, s32[640]{0:T(1024)}, u32[]{:S(2)}) copy-start(s32[640]{0:T(1024)} %param.10) | copy-start | bytes 7684
  320.5 10.7 %all-to-all-start = ((bf16[16,10,384]{2,1,0:T(8,128)(2,1)}), bf16[16,10,384]{2,1,0:T(8,128)(2,1)S(1)}, u32[]{:S(2)}, u32[]{:S(2)}) async-start(bf16[16,10,384]{2,1,0:T(8,128)(2,1)} %reshape.65), calls=%async_computation | async-start | bytes 393216 | tf_op jit(solution)/shard_map/all_to_all | solution.py:71
Sparse Core Ops, SparseCore 0:
  13.7 229.3 all-reduce.4
  319.7 125.9 all-reduce.6
where the time goes:
time: 455 us; the launch traced here: 454 us
  waiting for transfers between devices  336 us (74%)
  blocking collectives  62.1 us (14%)
  matrix products  18.3 us (4%)
  between operations  14.8 us (3%)
  other arithmetic  12.9 us (3%)
  local copies, waits for them, and re-layouts  6.5 us (1%)
    psum x1, waiting for transfers between devices, on_device(): lax.psum(lax.dot_general(picked, table, (((1,), (1,)), ((), ())), preferr...  227 us
    unnamed x3, waiting for transfers between devices  103 us
    pmax x1, blocking collectives, combine_stats(): largest = lax.pmax(local_max, 'vocab')  33.1 us
    psum x1, blocking collectives, combine_stats(): totals = lax.psum((local_exp, local_target), 'vocab')  29 us
  transfers between devices with their start and end apart: 3, of which 3 were waited for; matrix products, arithmetic and copies ran while one was open for 3% of the time, Pallas kernels for 0%

commit v1 on v0

v1 whole, which is shorter than its diff:
```python
import functools

import jax
import jax.numpy as jnp
from jax import lax
from jax.experimental import pallas as pl
from jax.experimental.pallas import tpu as pltpu
from jax.sharding import PartitionSpec as P

logit_scale = 0.8333333
MESH = pl.DeviceIdType.MESH
LANES = 128
PHASES = ((0, 24), (24, 16))
SKEW = 2
CHUNKS = 4


def head_kernel(
    nz, nv,
    targets_ref, rows_ref, owners_ref, ig_ref, hidden_hbm, table_hbm,
    loss_ref, hg_ref, tg_hbm,
    hidc, tabc, tab, part, ring_a, ring_b, lg_a, lg_b, g_all, gn_a, gn_b, acc,
    hgs_a, hgs_b, hgr_a, hgr_b, igs, st1_a, st1_b, st2_a, st2_b,
    load_sem, give_send, give_recv, rs_send, rs_recv, ag_send, ag_recv, core_send, core_recv,
    st1_send, st1_recv, st2_send, st2_recv, ig_send, ig_recv, hg_send, hg_recv, out_sem,
):
    half_ring = nz // 2
    tokens, width = hidden_hbm.shape
    vocab_part = table_hbm.shape[0]
    half = vocab_part // 2
    quarter = half // 2
    block = tokens // nz
    ring = (ring_a, ring_b)
    lg = (lg_a, lg_b)
    gn = (gn_a, gn_b)
    hgs = (hgs_a, hgs_b)
    hgr = (hgr_a, hgr_b)
    st1 = (st1_a, st1_b)
    st2 = (st2_a, st2_b)
    dp = lax.axis_index("dp")
    v = lax.axis_index("vocab")
    z = dp // 2
    c = dp % 2
    near = {"dp": z * 2 + (1 - c)}
    step_to = tuple({"dp": ((z + nz + sign) % nz) * 2 + c} for sign in (1, -1))
    signs = (1, -1)

    def at_z(offset):
        return (z + offset + 2 * nz) % nz

    def peer(i):
        return (v + i) % nv

    def remote(src, dst, send, recv, device):
        return pltpu.make_async_remote_copy(
            src_ref=src, dst_ref=dst, send_sem=send, recv_sem=recv,
            device_id=device, device_id_type=MESH,
        )

    my_lanes = pl.ds(pl.multiple_of(c * width, LANES), width)
    my_half = pl.ds(pl.multiple_of(c * half, half), half)
    loads = [
        pltpu.make_async_copy(hidden_hbm, hidc.at[:, my_lanes], load_sem.at[0]),
        pltpu.make_async_copy(table_hbm.at[my_half], tabc.at[:, my_lanes], load_sem.at[1]),
        pltpu.make_async_copy(table_hbm, tab, load_sem.at[2]),
    ]
    for copy in loads:
        copy.start()
    barrier = pltpu.get_barrier_semaphore()
    for device in (near, step_to[0], step_to[1]):
        pl.semaphore_signal(barrier, inc=1, device_id=device, device_id_type=MESH)

    @pl.loop(1, nv)
    def _(i):
        pl.semaphore_signal(barrier, inc=1, device_id={"vocab": peer(i)}, device_id_type=MESH)

    pl.semaphore_wait(barrier, 3 + nv - 1)

    chunk = half // CHUNKS
    gives = [remote(hidden_hbm, hidc.at[:, my_lanes], give_send.at[0], give_recv.at[0], near)]
    for j in range(CHUNKS):
        its = pl.ds(pl.multiple_of((1 - c) * half + j * chunk, chunk), chunk)
        gives.append(
            remote(
                table_hbm.at[its],
                tabc.at[pl.ds(j * chunk, chunk), my_lanes],
                give_send.at[1 + j],
                give_recv.at[1 + j],
                near,
            )
        )
    for copy in gives:
        copy.start()
    sent = list(gives)

    def rs_copy(p, h, way, s):
        first, count = PHASES[p]
        cols = pl.ds(h * quarter, quarter)
        return remote(
            part.at[at_z(signs[way] * (half_ring - s)), pl.ds(first, count), cols],
            ring[p].at[way, s, :, cols],
            rs_send.at[p, h, way, s],
            rs_recv.at[p, h, way, s],
            step_to[way],
        )

    def rs_exists(h, way, s):
        return s > 0 or h == way

    def rs_start(p, h, way, s):
        copy = rs_copy(p, h, way, s)
        copy.start()
        sent.append(copy)

    def rs_advance(p, h, way, s):
        first, count = PHASES[p]
        if rs_exists(h, way, s):
            rs_copy(p, h, way, s).wait_recv()
            d = at_z(signs[way] * (half_ring - 1 - s))
            spot = (d, pl.ds(first, count), pl.ds(h * quarter, quarter))
            part[spot] = part[spot] + ring[p][way, s, :, h * quarter : (h + 1) * quarter]
        if s + 1 < half_ring:
            rs_start(p, h, way, s + 1)

    def rs_step(p, s):
        for h in range(2):
            for way in range(2):
                if rs_exists(h, way, s):
                    rs_advance(p, h, way, s)

    loads[0].wait()
    loads[1].wait()
    gives[0].wait_recv()
    for j in range(CHUNKS):
        gives[1 + j].wait_recv()
        cols = slice(j * chunk, (j + 1) * chunk)
        part[:, :, cols] = lax.dot_general(
            hidc[...], tabc[cols, :], (((1,), (1,)), ((), ())),
            preferred_element_type=jnp.float32,
        ).reshape(nz, block, chunk)
        if j == CHUNKS // 2 - 1:
            rs_start(0, 0, 0, 0)
    rs_start(0, 1, 1, 0)
    if half_ring > 1:
        rs_start(0, 1, 0, 1)
        rs_start(0, 0, 1, 1)

    def rs_open(p):
        rs_start(p, 0, 0, 0)
        rs_start(p, 1, 1, 0)
        if half_ring > 1:
            rs_start(p, 1, 0, 1)
            rs_start(p, 0, 1, 1)

    igs[v] = ig_ref[...].astype(jnp.float32)

    def ig_copy(i):
        to = peer(i)
        return remote(igs.at[v], igs.at[v], ig_send.at[i], ig_recv.at[i], {"vocab": to})

    @pl.loop(1, nv)
    def _(i):
        ig_copy(i).start()

    def wait_ig():
        @pl.loop(1, nv)
        def _(i):
            ig_copy(i).wait_recv()

    piece = vocab_part // 8

    def embed(j):
        ids = owners_ref[...] * vocab_part + rows_ref[...] - (v * vocab_part + j * piece)
        chosen = (lax.broadcasted_iota(jnp.int32, (piece, tokens), 0) == ids).astype(jnp.float32)
        acc[pl.ds(j * piece, piece), :] = jnp.dot(
            chosen.astype(jnp.bfloat16),
            igs[...].reshape(tokens, width).astype(jnp.bfloat16),
            preferred_element_type=jnp.float32,
        )

    lane = lax.broadcasted_iota(jnp.int32, (1, LANES), 1)

    def aimed_of(p):
        first, count = PHASES[p]
        token = lax.broadcasted_iota(jnp.int32, (count, tokens), 0) + (z * block + first)
        here = lax.broadcasted_iota(jnp.int32, (count, tokens), 1) == token
        wanted = jnp.sum(
            jnp.where(here, targets_ref[...].astype(jnp.float32), 0.0), axis=1, keepdims=True
        ).astype(jnp.int32)
        column = lax.broadcasted_iota(jnp.int32, (count, half), 1) + (v * vocab_part + c * half)
        return column == wanted

    def st1_copy(p):
        return remote(st1[p].at[0], st1[p].at[1], st1_send.at[p], st1_recv.at[p], near)

    def st2_copy(p, i):
        return remote(
            st2[p].at[v], st2[p].at[v], st2_send.at[p, i], st2_recv.at[p, i], {"vocab": peer(i)}
        )

    def pack(m, s, t):
        return jnp.where(lane == 0, m, jnp.where(lane == 1, s, t))

    def stats_local(p):
        first, count = PHASES[p]
        last = half_ring - 1
        for h in range(2):
            for way in range(2):
                if rs_exists(h, way, last):
                    rs_copy(p, h, way, last).wait_recv()
        total = part[z, pl.ds(first, count), :]
        if last > 0:
            total = total + ring[p][0, last] + ring[p][1, last]
            x = logit_scale * total
            lg[p][...] = x
        else:
            lg[p][:, :quarter] = logit_scale * (total[:, :quarter] + ring[p][0, 0, :, :quarter])
            lg[p][:, quarter:] = logit_scale * (total[:, quarter:] + ring[p][1, 0, :, quarter:])
            x = lg[p][...]
        m = jnp.max(x, axis=1, keepdims=True)
        s = jnp.sum(jnp.exp(x - m), axis=1, keepdims=True)
        t = jnp.sum(jnp.where(aimed_of(p), x, 0.0), axis=1, keepdims=True)
        st1[p][0] = pack(m, s, t)
        st1_copy(p).start()

    def stats_core(p):
        st1_copy(p).wait_recv()
        one, two = st1[p][0], st1[p][1]
        m1, m2 = one[:, 0:1], two[:, 0:1]
        m = jnp.maximum(m1, m2)
        s = one[:, 1:2] * jnp.exp(m1 - m) + two[:, 1:2] * jnp.exp(m2 - m)
        st2[p][v] = pack(m, s, one[:, 2:3] + two[:, 2:3])

        @pl.loop(1, nv)
        def _(i):
            st2_copy(p, i).start()

    def stats_final(p):
        first, count = PHASES[p]

        @pl.loop(1, nv)
        def _(i):
            st2_copy(p, i).wait_recv()

        every = st2[p][...]
        m, s, t = every[:, :, 0:1], every[:, :, 1:2], every[:, :, 2:3]
        top = jnp.max(m, axis=0)
        log_total = top + jnp.log(jnp.sum(s * jnp.exp(m - top[None]), axis=0))
        loss_ref[pl.ds(first, count), :] = jnp.broadcast_to(
            log_total - jnp.sum(t, axis=0), (count, LANES)
        )
        grads = jnp.exp(lg[p][...] - log_total) - aimed_of(p).astype(jnp.float32)
        for g in range(count // 8):
            eight = grads[g * 8 : (g + 1) * 8]
            g_all[c, z, first // 8 + g] = jnp.concatenate(
                [eight[:, :quarter], eight[:, quarter:]], axis=0
            ).astype(jnp.bfloat16)

    def ag_copy(p, way, s):
        first, count = PHASES[p]
        d = at_z(-signs[way] * s)
        groups = pl.ds(first // 8, count // 8)
        lanes = pl.ds(0, quarter)
        if s == half_ring - 1:
            lanes = pl.ds(way * (quarter // 2), quarter // 2)
        ref = g_all.at[c, d, groups, :, lanes]
        return remote(ref, ref, ag_send.at[p, way, s], ag_recv.at[p, way, s], step_to[way])

    def core_copy(p, k, d, side):
        first, count = PHASES[p]
        ref = g_all.at[side, d, pl.ds(first // 8, count // 8)]
        return remote(ref, ref, core_send.at[p, k], core_recv.at[p, k], near)

    def core_block(k):
        if k == 0:
            return z
        if k == nz - 1:
            return at_z(half_ring)
        return at_z(-signs[(k - 1) % 2] * ((k - 1) // 2 + 1))

    def core_start(p, k):
        copy = core_copy(p, k, core_block(k), c)
        copy.start()
        sent.append(copy)

    def ag_start(p, way, s):
        copy = ag_copy(p, way, s)
        copy.start()
        sent.append(copy)

    def ag_open(p):
        for way in range(2):
            ag_start(p, way, 0)
        core_start(p, 0)

    def ag_step(p, s):
        for way in range(2):
            ag_copy(p, way, s).wait_recv()
            if s + 1 < half_ring:
                ag_start(p, way, s + 1)
                core_start(p, 1 + 2 * s + way)
        if s + 1 == half_ring:
            core_start(p, nz - 1)

    def ag_close(p):
        first, count = PHASES[p]
        for k in range(nz):
            core_copy(p, k, core_block(k), 1 - c).wait_recv()
        for side in range(2):
            x = g_all[side, :, first // 8 : (first + count) // 8].astype(jnp.float32)
            for part_of in range(2):
                cols = slice(side * half + part_of * quarter, side * half + (part_of + 1) * quarter)
                gn[p][:, cols] = (
                    x[:, :, 8 * part_of : 8 * part_of + 8, :]
                    .reshape(nz * count, quarter)
                    .astype(jnp.bfloat16)
                )

    def hg_copy(p, i):
        to = peer(i)
        return remote(
            hgs[p].at[to], hgr[p].at[v], hg_send.at[p, i], hg_recv.at[p, i], {"vocab": to}
        )

    def hg_start(p):
        count = PHASES[p][1]
        hgs[p][...] = jnp.dot(
            gn[p][...], tab[...], preferred_element_type=jnp.float32
        ).reshape(nv, count, width)
        hgr[p][v] = hgs[p][v]

        @pl.loop(1, nv)
        def _(i):
            hg_copy(p, i).start()

    def hg_wait(p):
        @pl.loop(1, nv)
        def _(i):
            hg_copy(p, i).wait_recv()

    def hidden_rows(p):
        first, count = PHASES[p]
        own = hidc[:, my_lanes].astype(jnp.float32).reshape(nz, block, width)
        return own[:, first : first + count].reshape(nz * count, width).astype(jnp.bfloat16)

    def head(p, j, own):
        spot = (pl.ds(j * piece, piece), slice(None))
        acc[spot] = acc[spot] + logit_scale * lax.dot_general(
            gn[p][:, j * piece : (j + 1) * piece], own, (((0,), (0,)), ((), ())),
            preferred_element_type=jnp.float32,
        )

    def out_copy(j):
        rows = pl.ds(j * piece, piece)
        return pltpu.make_async_copy(acc.at[rows], tg_hbm.at[rows], out_sem.at[j])

    filler = [functools.partial(embed, j) for j in range(8)]
    for slot in range(half_ring - 1 + SKEW):
        if slot < half_ring - 1:
            rs_step(0, slot)
        elif slot == half_ring - 1:
            stats_local(0)
        if slot == SKEW:
            rs_open(1)
        if slot >= SKEW:
            rs_step(1, slot - SKEW)
        if slot == half_ring:
            stats_core(0)
        if slot == 1:
            wait_ig()
        if slot >= 1 and filler:
            filler.pop(0)()
            if slot >= 2 and filler:
                filler.pop(0)()
    while filler:
        filler.pop(0)()
    if SKEW < 1:
        stats_local(0)
    if SKEW < 2:
        stats_core(0)
    stats_local(1)
    stats_final(0)
    ag_open(0)
    stats_core(1)
    for s in range(half_ring):
        ag_step(0, s)
        if s == min(1, half_ring - 1):
            stats_final(1)
            ag_open(1)
        if s >= 2:
            ag_step(1, s - 2)
    loads[2].wait()
    own = hidden_rows(0)
    for s in range(max(half_ring - 2, 0), half_ring):
        ag_step(1, s)
        if s == max(half_ring - 2, 0):
            ag_close(0)
            hg_start(0)
    for j in range(8):
        head(0, j, own)
    ag_close(1)
    hg_start(1)
    own = hidden_rows(1)
    for j in range(8):
        head(1, j, own)
        out_copy(j).start()
    for p in range(2):
        hg_wait(p)
    pieces = []
    for p in range(2):
        pieces.append(jnp.sum(hgr[p][...], axis=0))
    hg_ref[...] = (logit_scale * jnp.concatenate(pieces, axis=0)).astype(jnp.bfloat16)

    for copy in sent:
        copy.wait_send()
    for p in range(2):
        st1_copy(p).wait_send()

    @pl.loop(1, nv)
    def _(i):
        ig_copy(i).wait_send()
        for p in range(2):
            st2_copy(p, i).wait_send()
            hg_copy(p, i).wait_send()

    for j in range(8):
        out_copy(j).wait()


def on_device(hidden, table, targets, owners, rows, input_grad):
    nz = lax.axis_size("dp") // 2
    nv = lax.axis_size("vocab")
    tokens, width = hidden.shape
    vocab_part = table.shape[0]
    half = vocab_part // 2
    block = tokens // nz
    half_ring = nz // 2
    counts = [count for _, count in PHASES]
    f32, bf16 = jnp.float32, jnp.bfloat16
    vmem = pl.BlockSpec(memory_space=pltpu.VMEM)
    hbm = pl.BlockSpec(memory_space=pl.ANY)
    dma = pltpu.SemaphoreType.DMA
    each = lambda shape, kind: [pltpu.VMEM(shape(count), kind) for count in counts]
    loss, hidden_grad, table_grad = pl.pallas_call(
        functools.partial(head_kernel, nz, nv),
        out_shape=(
            jax.ShapeDtypeStruct((block, LANES), f32),
            jax.ShapeDtypeStruct((block, width), bf16),
            jax.ShapeDtypeStruct((vocab_part, width), f32),
        ),
        in_specs=[vmem, vmem, vmem, vmem, hbm, hbm],
        out_specs=(vmem, vmem, hbm),
        scratch_shapes=[
            pltpu.VMEM((tokens, 2 * width), bf16),
            pltpu.VMEM((half, 2 * width), bf16),
            pltpu.VMEM((vocab_part, width), bf16),
            pltpu.VMEM((nz, block, half), f32),
            *each(lambda n: (2, half_ring, n, half), f32),
            *each(lambda n: (n, half), f32),
            pltpu.VMEM((2, nz, block // 8, 16, half // 2), bf16),
            *each(lambda n: (nz * n, vocab_part), bf16),
            pltpu.VMEM((vocab_part, width), f32),
            *each(lambda n: (nv, n, width), f32),
            *each(lambda n: (nv, n, width), f32),
            pltpu.VMEM((nv, block, width), f32),
            *each(lambda n: (2, n, LANES), f32),
            *each(lambda n: (nv, n, LANES), f32),
            dma((3,)),
            dma((1 + CHUNKS,)),
            dma((1 + CHUNKS,)),
            dma((2, 2, 2, half_ring)),
            dma((2, 2, 2, half_ring)),
            dma((2, 2, half_ring)),
            dma((2, 2, half_ring)),
            dma((2, nz)),
            dma((2, nz)),
            dma((2,)),
            dma((2,)),
            dma((2, nv)),
            dma((2, nv)),
            dma((nv,)),
            dma((nv,)),
            dma((2, nv)),
            dma((2, nv)),
            dma((8,)),
        ],
        compiler_params=pltpu.CompilerParams(
            collective_id=0, has_side_effects=True, vmem_limit_bytes=56 * 1024 * 1024
        ),
        name="head",
    )(
        targets.reshape(1, tokens), rows.reshape(1, tokens), owners.reshape(1, tokens),
        input_grad, hidden, table,
    )
    token_loss = lax.dynamic_slice(
        loss[:, 0], ((lax.axis_index("dp") % 2) * (block // 2),), (block // 2,)
    )
    return (token_loss, hidden_grad, table_grad)


def solution(mesh):
    return jax.shard_map(
        on_device,
        mesh=mesh,
        in_specs=(P(None, "dp"), P("vocab", "dp"), P(), P(), P(), P("vocab", "dp")),
        out_specs=(P("dp"), P("vocab", "dp"), P("vocab", "dp")),
        check_vma=False,
    )
```

time: 455 us -> 127 us (0.28)
  waiting for transfers between devices: 336 us -> 0 us
  Pallas kernels: 0 us -> 117 us
  blocking collectives: 62.1 us -> 0 us
  matrix products: 18.3 us -> 0 us
  between operations: 14.8 us -> 0.66 us
  other arithmetic: 12.9 us -> 0 us
    psum x1 -> x0, waiting for transfers between devices: 227 us -> none  [on_device(): lax.psum(lax.dot_general(picked, table, (((1,), (1,)), ((), ())), preferr...]
    pallas_call x0 -> x1, Pallas kernels: none -> 117 us  [on_device(): pl.pallas_call(functools.partial(head_kernel, nz, nv), out_shape=(jax.Sha...]
    unnamed x3 -> x0, waiting for transfers between devices: 103 us -> none
    pmax x1 -> x0, blocking collectives: 33.1 us -> none  [combine_stats(): largest = lax.pmax(local_max, 'vocab')]
    psum x1 -> x0, blocking collectives: 29 us -> none  [combine_stats(): totals = lax.psum((local_exp, local_target), 'vocab')]
    dot_general x5 -> x0, matrix products: 18.3 us -> none  [the longest x1 5.58 us: on_device(): lax.dot_general(slot_rows, incoming.reshape(slot_total, width_part), (((0...]
    all_to_all x1 -> x0, waiting for transfers between devices: 5.2 us -> none  [on_device(): lax.all_to_all(outgoing.reshape(vocab_count, capacity, width_part), 'voca...]
    convert_element_type x2 -> x0, other arithmetic: 4.78 us -> none  [the longest x1 3.33 us: on_device(): (jnp.exp(logits - log_total[:, None]) - aimed.astype(jnp.float32)).astype...]
  transfers between devices with their start and end apart: 3 -> 0, of which waited for: 3 -> 0; matrix products, arithmetic and copies ran while one was open for 3% -> 0% of each run, Pallas kernels for 0% -> 0%
where the time goes in v1:
time: 127 us
  Pallas kernels  117 us (92%)
  local copies, waits for them, and re-layouts  9 us (7%)
    pallas_call x1, Pallas kernels, on_device(): pl.pallas_call(functools.partial(head_kernel, nz, nv), out_shape=(jax.Sha...  117 us
    unnamed x2, local copies, waits for them, and re-layouts  5.12 us

profile of v1, /device:TPU:1, one launch (start us, length us, event | category | flops | bytes accessed | tf_op | source)
XLA Modules:
  0.0 126.7 jit_solution(6745808830358088347)
XLA Ops:
  0.6 1.3 %reshape.16.targets_ref = s32[1,640]{1,0:T(1,128)} reshape(s32[640]{0:T(1024)} %param.8) | data formatting | bytes 5120 | tf_op jit(solution)/shard_map/reshape | solution.py:492
  1.9 1.3 reshape.17.rows_ref
  3.2 117.0 %head.1 = (f32[40,128]{1,0:T(8,128)}, bf16[40,384]{1,0:T(8,128)(2,1)}, f32[2048,384]{1,0:T(8,128)}) custom-call(s32[1,640]{1,0:T(1,128)} %reshape.16.targets_ref, s32[1,640]{1,0:T(1,128)} %reshape.17.rows_ref, s32[1,640]{1,0:T(1,128)} %bitcast.3, bf16[40,384]{1,0:T(8,128)(2,1)} %ig_ref.1, bf16[640,384]{1,0:T(8,128)(2,1)} %hidden_hbm.1, ...), custom_call_target="tpu_custom_call" | custom-call | tf_op jit(solution)/shard_map/head/pallas_call | solution.py:444
  120.2 1.3 %dynamic-slice_reduce_fusion = f32[20]{0:T(128)} fusion(f32[40,1]{1,0:T(8,128)} %bitcast.2, s32[]{:T(128)S(6)} %select_n.11), kind=kLoop, calls=%fused_computation | loop fusion | bytes 164 | tf_op jit(solution)/shard_map/dynamic_slice | solution.py:495
  121.5 1.4 %copy.11 = bf16[40,384]{1,0:T(8,128)(2,1)} copy(bf16[40,384]{1,0:T(8,128)(2,1)} %get-tuple-element.13) | data formatting | bytes 61440
  122.9 3.8 %copy.12 = f32[2048,384]{1,0:T(8,128)} copy(f32[2048,384]{1,0:T(8,128)} %get-tuple-element.14) | data formatting | bytes 6291456

commit v2 on v0

v2 whole, which is shorter than its diff:
```python
import functools

import jax
import jax.numpy as jnp
from jax import lax
from jax.experimental import pallas as pl
from jax.experimental.pallas import tpu as pltpu
from jax.sharding import PartitionSpec as P

logit_scale = 0.8333333
MESH = pl.DeviceIdType.MESH
LANES = 128
CHUNKS = 4
PAD = 8
PIECES = 8
AG_TREE = {7: 5}
AG_ORDER = (1, 2, 3, 4, 5, 6, 7, 8)


def head_kernel(
    nz, nv,
    targets_ref, rows_ref, owners_ref, ig_ref, hidden_hbm, table_hbm,
    loss_ref, hg_ref, tg_hbm,
    hidc, tabc, tab, part, ring, g_all, gn, acc, hid32, hid_near, tcol,
    hgs, hgr, igs, mst, st1, st2, stz,
    load_sem, give_send, give_recv, rs_send, rs_recv, ag_send, ag_recv, core_send, core_recv,
    st1_send, st1_recv, st2_send, st2_recv, stz_send, stz_recv, ig_send, ig_recv,
    hg_send, hg_recv, out_sem,
):
    half_ring = nz // 2
    tree = {b: AG_TREE.get(b, b - 1) if nz == 16 else b - 1 for b in range(1, half_ring + 1)}
    tokens, width = hidden_hbm.shape
    vocab_part = table_hbm.shape[0]
    half = vocab_part // 2
    quarter = half // 2
    block = tokens // nz
    groups = block // 8
    dp = lax.axis_index("dp")
    v = lax.axis_index("vocab")
    z = dp // 2
    c = dp % 2
    signs = (1, -1)

    def at_z(offset):
        return (z + offset + 2 * nz) % nz

    def peer(i):
        return (v + i) % nv

    def zdev(offset):
        return {"dp": at_z(offset) * 2 + c}

    near = {"dp": z * 2 + (1 - c)}
    step_to = tuple(zdev(sign) for sign in signs)

    def nearby(k):
        return at_z(jnp.where(k % 2 == 1, -((k + 1) // 2), k // 2))

    def remote(src, dst, send, recv, device):
        return pltpu.make_async_remote_copy(
            src_ref=src, dst_ref=dst, send_sem=send, recv_sem=recv,
            device_id=device, device_id_type=MESH,
        )

    my_lanes = pl.ds(pl.multiple_of(c * width, LANES), width)
    my_half = pl.ds(pl.multiple_of(c * half, half), half)
    loads = [
        pltpu.make_async_copy(hidden_hbm, hidc.at[:, my_lanes], load_sem.at[0]),
        pltpu.make_async_copy(table_hbm.at[my_half], tabc.at[:, my_lanes], load_sem.at[1]),
        pltpu.make_async_copy(table_hbm, tab, load_sem.at[2]),
    ]
    barrier = pltpu.get_barrier_semaphore()
    pl.semaphore_signal(barrier, inc=1, device_id=near, device_id_type=MESH)
    for copy in loads:
        copy.start()

    @pl.loop(1, nz)
    def _(i):
        pl.semaphore_signal(barrier, inc=1, device_id=zdev(i), device_id_type=MESH)

    @pl.loop(1, nv)
    def _(i):
        pl.semaphore_signal(barrier, inc=1, device_id={"vocab": peer(i)}, device_id_type=MESH)

    pl.semaphore_wait(barrier, nz + nv - 1)

    chunk = half // CHUNKS
    gives = [remote(hidden_hbm, hidc.at[:, my_lanes], give_send.at[0], give_recv.at[0], near)]
    for j in range(CHUNKS):
        its = pl.ds(pl.multiple_of((1 - c) * half + j * chunk, chunk), chunk)
        gives.append(
            remote(
                table_hbm.at[its],
                tabc.at[pl.ds(j * chunk, chunk), my_lanes],
                give_send.at[1 + j],
                give_recv.at[1 + j],
                near,
            )
        )
    for copy in gives:
        copy.start()

    def rs_copy(way, s, g):
        rows = pl.ds(pl.multiple_of(g * 8, 8), 8)
        cols = pl.ds(0, half) if s else pl.ds(way * quarter, quarter)
        return remote(
            part.at[at_z(signs[way] * (half_ring - s)), rows, cols],
            ring.at[way, s, rows, cols],
            rs_send.at[way, min(s, 1)],
            rs_recv.at[way, s, g],
            step_to[way],
        )

    def rs_open(way):
        @pl.loop(0, groups)
        def _(g):
            rs_copy(way, 0, g).start()

    def rs_step(s):
        @pl.loop(0, groups)
        def _(g):
            rows = pl.ds(pl.multiple_of(g * 8, 8), 8)
            for way in range(2):
                cols = pl.ds(0, half) if s else pl.ds(way * quarter, quarter)
                rs_copy(way, s, g).wait_recv()
                spot = (at_z(signs[way] * (half_ring - 1 - s)), rows, cols)
                part[spot] = part[spot] + ring[way, s, rows, cols]
                rs_copy(way, s + 1, g).start()

    loads[0].wait()
    loads[1].wait()
    gives[0].wait_recv()
    for j in range(CHUNKS):
        gives[1 + j].wait_recv()
        cols = slice(j * chunk, (j + 1) * chunk)
        part[:, :, cols] = lax.dot_general(
            hidc[...], tabc[cols, :], (((1,), (1,)), ((), ())),
            preferred_element_type=jnp.float32,
        ).reshape(nz, block, chunk)
        if j == CHUNKS // 2 - 1:
            rs_open(0)
    rs_open(1)

    igs[v] = ig_ref[...].astype(jnp.float32)

    def ig_copy(i):
        return remote(igs.at[v], igs.at[v], ig_send, ig_recv, {"vocab": peer(i)})

    @pl.loop(1, nv)
    def _(i):
        ig_copy(i).start()

    def wait_ig():
        rest = igs.at[pl.ds(1, nv - 1)]
        remote(rest, rest, ig_send, ig_recv, near).wait_recv()

    piece = vocab_part // 8

    def embed(j):
        ids = owners_ref[...] * vocab_part + rows_ref[...].reshape(1, tokens) - (v * vocab_part + j * piece)
        chosen = (lax.broadcasted_iota(jnp.int32, (piece, tokens), 0) == ids).astype(jnp.float32)
        acc[pl.ds(j * piece, piece), :] = jnp.dot(
            chosen.astype(jnp.bfloat16),
            igs[...].reshape(tokens, width).astype(jnp.bfloat16),
            preferred_element_type=jnp.float32,
        )

    def own_rows():
        hid32[...] = hidc[:, my_lanes].astype(jnp.float32).reshape(nz, block, width)

    def pair_rows():
        @pl.loop(0, nz // 2)
        def _(j):
            two = jnp.concatenate([hid32[nearby(2 * j)], hid32[nearby(2 * j + 1)]], axis=0)
            rows = pl.ds(pl.multiple_of(j * 2 * block, 16), 2 * block)
            hid_near[rows, :] = two.astype(jnp.bfloat16)

    def target_columns():
        @pl.loop(0, nz)
        def _(d):
            token = lax.broadcasted_iota(jnp.int32, (block, tokens), 0) + d * block
            here = lax.broadcasted_iota(jnp.int32, (block, tokens), 1) == token
            wanted = jnp.sum(
                jnp.where(here, targets_ref[...].reshape(1, tokens).astype(jnp.float32), 0.0), axis=1, keepdims=True
            )
            tcol[d] = jnp.broadcast_to(wanted.astype(jnp.int32), (block, LANES))

    lane = lax.broadcasted_iota(jnp.int32, (1, LANES), 1)
    sub = lax.broadcasted_iota(jnp.int32, (8, LANES), 0)
    eye = lax.broadcasted_iota(jnp.int32, (block, LANES), 0) == lax.broadcasted_iota(
        jnp.int32, (block, LANES), 1
    )
    first_col = v * vocab_part

    def as_row(x):
        return jnp.sum(jnp.where(eye, x, 0.0), axis=0, keepdims=True)

    def as_col(x):
        return jnp.sum(jnp.where(eye, x, 0.0), axis=1, keepdims=True)

    st1_copy = remote(st1.at[0], st1.at[1], st1_send, st1_recv, near)

    def st2_copy(i):
        return remote(st2.at[v], st2.at[v], st2_send, st2_recv, {"vocab": peer(i)})

    def stz_copy(i):
        return remote(stz.at[z], stz.at[z], stz_send, stz_recv, zdev(i))

    def pack(a, b, c):
        return jnp.where(sub == 0, a, jnp.where(sub == 1, b, c))

    def ag_copy(way, b, g):
        a = tree[b]
        d = at_z(-signs[way] * a)
        lanes = pl.ds(0, quarter)
        if b == half_ring:
            lanes = pl.ds(way * (quarter // 2), quarter // 2)
        ref = g_all.at[c, d, g, :, lanes]
        return remote(
            ref, ref, ag_send.at[way, b // half_ring], ag_recv.at[way, b - 1, g],
            zdev(signs[way] * (b - a)),
        )

    def ag_on(way, a, g):
        for b in sorted(tree):
            if tree[b] == a:
                ag_copy(way, b, g).start()

    def core_copy(k, side):
        ref = g_all.at[side, nearby(k)]
        return remote(ref, ref, core_send, core_recv.at[k], near)

    def ag_step(b):
        @pl.loop(0, groups)
        def _(g):
            for way in range(2):
                ag_copy(way, b, g).wait_recv()
                ag_on(way, b, g)

        core_copy(2 * b - 1, c).start()
        if b < half_ring:
            core_copy(2 * b, c).start()

    def finish_logits():
        last = half_ring - 1

        @pl.loop(0, groups)
        def _(g):
            rows = pl.ds(pl.multiple_of(g * 8, 8), 8)
            for way in range(2):
                rs_copy(way, last, g).wait_recv()
            x = logit_scale * (part[z, rows, :] + ring[0, last, rows, :] + ring[1, last, rows, :])
            m = jnp.max(x, axis=1, keepdims=True)
            e = jnp.exp(x - m)
            g_all[c, z, g] = jnp.concatenate([e[:, :quarter], e[:, quarter:]], axis=0).astype(
                jnp.bfloat16
            )
            for way in range(2):
                ag_on(way, 0, g)
            column = lax.broadcasted_iota(jnp.int32, (8, half), 1) + (first_col + c * half)
            aimed = column == tcol[z, rows, 0:1]
            t = jnp.sum(jnp.where(aimed, x, 0.0), axis=1, keepdims=True)
            mst[rows, :] = jnp.where(
                lane == 0, m, jnp.where(lane == 1, jnp.sum(e, axis=1, keepdims=True), t)
            )

        st1[0] = pack(as_row(mst[:, 0:1]), as_row(mst[:, 1:2]), as_row(mst[:, 2:3]))
        st1_copy.start()
        core_copy(0, c).start()

    def stats_core():
        st1_copy.wait_recv()
        one, two = st1[0], st1[1]
        m1, m2 = one[0:1], two[0:1]
        m = jnp.maximum(m1, m2)
        s = one[1:2] * jnp.exp(m1 - m) + two[1:2] * jnp.exp(m2 - m)
        st2[v] = pack(m, s, one[2:3] + two[2:3])

        @pl.loop(1, nv)
        def _(i):
            st2_copy(i).start()

    def stats_final():
        rest = st2.at[pl.ds(1, nv - 1)]
        remote(rest, rest, st2_send, st2_recv, near).wait_recv()

        every = st2[...]
        m, s, t = every[:, 0], every[:, 1], every[:, 2]
        top = jnp.max(m, axis=0, keepdims=True)
        log_total = top + jnp.log(jnp.sum(s * jnp.exp(m - top), axis=0, keepdims=True))
        target = jnp.sum(t, axis=0, keepdims=True)
        mine = jnp.exp(st1[0, 0:1, :] - log_total)
        other = jnp.exp(st1[1, 0:1, :] - log_total)
        stz[z] = pack(
            jnp.where(c == 0, mine, other),
            jnp.where(c == 0, other, mine),
            jnp.exp(target - log_total) - 1.0,
        )

        @pl.loop(1, nz)
        def _(i):
            stz_copy(i).start()

        pick = lax.broadcasted_iota(jnp.int32, (block, LANES), 0) == (
            lax.broadcasted_iota(jnp.int32, (block, LANES), 1) + c * (block // 2)
        )
        loss_ref[...] = jnp.broadcast_to(
            jnp.sum(jnp.where(pick, as_col(log_total - target), 0.0), axis=0, keepdims=True),
            (8, LANES),
        )

    def stz_wait():
        rest = stz.at[pl.ds(1, nz - 1)]
        remote(rest, rest, stz_send, stz_recv, near).wait_recv()

    def core_wait(first, last):
        for k in range(first, last):
            core_copy(k, 1 - c).wait_recv()

    def gradients(first, last):
        @pl.loop(first // 2, last // 2)
        def _(j):
            rows = pl.ds(pl.multiple_of(j * 2 * block, 16), 2 * block)
            ds = [nearby(2 * j), nearby(2 * j + 1)]
            factors = [[as_col(stz[d, r : r + 1, :]) for r in range(3)] for d in ds]
            wanted = [tcol[d, :, 0:1] - first_col for d in ds]
            for side in range(2):
                for q in range(2):
                    base = side * half + q * quarter
                    column = lax.broadcasted_iota(jnp.int32, (block, quarter), 1) + base
                    both = []
                    for d, f, w in zip(ds, factors, wanted):
                        e = g_all[side, d].astype(jnp.float32)[:, 8 * q : 8 * q + 8, :]
                        both.append(
                            jnp.where(column == w, f[2], e.reshape(block, quarter) * f[side])
                        )
                    gn[rows, base : base + quarter] = jnp.concatenate(both, axis=0).astype(
                        jnp.bfloat16
                    )

    def hg_copy(k):
        to = nearby(k)
        return remote(
            hgs.at[k], hgr.at[v], hg_send, hg_recv, {"vocab": to}
        )

    def hidden_terms(first, last):
        if first == last:
            return
        terms = jnp.dot(
            gn[first * block : last * block, :], tab[...], preferred_element_type=jnp.float32
        ).reshape(last - first, block, width)
        low = jnp.concatenate([terms, jnp.zeros((last - first, PAD, width), jnp.float32)], axis=1)
        hgs[first:last] = low.astype(jnp.bfloat16)

        @pl.loop(first, last)
        def _(k):
            @pl.when(nearby(k) != v)
            def _():
                hg_copy(k).start()

    def hg_finish():
        offset = (v - z + nz + half_ring) % nz - half_ring
        k = jnp.where(offset < 0, -2 * offset - 1, 2 * offset)
        hgr[v] = hgs[k]

        rest = hgr.at[pl.ds(1, nv - 1)]
        remote(rest, rest, hg_send, hg_recv, near).wait_recv()
        hg_ref[...] = (
            logit_scale * jnp.sum(hgr[...].astype(jnp.float32)[:, :block], axis=0)
        ).astype(jnp.bfloat16)

    def head(j):
        spot = (pl.ds(j * piece, piece), slice(None))
        acc[spot] = acc[spot] + logit_scale * lax.dot_general(
            gn[:, j * piece : (j + 1) * piece], hid_near[...], (((0,), (0,)), ((), ())),
            preferred_element_type=jnp.float32,
        )

    def out_copy(j):
        rows = pl.ds(j * piece, piece)
        return pltpu.make_async_copy(acc.at[rows], tg_hbm.at[rows], out_sem.at[j])

    filler = [target_columns, own_rows, pair_rows, wait_ig]
    filler = filler + [functools.partial(embed, j) for j in range(8)]
    for s in range(half_ring - 1):
        rs_step(s)
        for _ in range(2):
            if filler:
                filler.pop(0)()
    while filler:
        filler.pop(0)()
    loads[2].wait()
    finish_logits()
    third = 3 * nz // 8 * 2
    stats_core()
    todo = {
        2: [stats_final],
        5: [stz_wait, lambda: core_wait(0, nz // 2), lambda: gradients(0, nz // 2)],
        7: [
            lambda: hidden_terms(0, nz // 2),
            lambda: core_wait(nz // 2, third),
            lambda: gradients(nz // 2, third),
        ],
    }
    for b in AG_ORDER if nz == 16 else range(1, half_ring + 1):
        ag_step(b)
        for act in todo.pop(b, []):
            act()
    for b in sorted(todo):
        for act in todo[b]:
            act()
    hidden_terms(nz // 2, third)
    core_wait(third, nz)
    gradients(third, nz)
    hidden_terms(third, nz)
    for j in range(8):
        head(j)
        out_copy(j).start()
    hg_finish()

    for copy in gives:
        copy.wait_send()
    st1_copy.wait_send()

    def all_sent(ref, sem):
        remote(ref, ref, sem, sem, near).wait_send()

    for way in range(2):
        all_sent(ring.at[way, 0, :, pl.ds(0, quarter)], rs_send.at[way, 0])
        all_sent(ring.at[way, pl.ds(1, half_ring - 1)], rs_send.at[way, 1])
        all_sent(g_all.at[c, pl.ds(1, half_ring - 1)], ag_send.at[way, 0])
        all_sent(g_all.at[c, 0, :, :, pl.ds(0, quarter // 2)], ag_send.at[way, 1])
    all_sent(g_all.at[c], core_send)
    all_sent(igs.at[pl.ds(1, nv - 1)], ig_send)
    all_sent(st2.at[pl.ds(1, nv - 1)], st2_send)
    all_sent(stz.at[pl.ds(1, nz - 1)], stz_send)
    all_sent(hgs.at[pl.ds(1, nv - 1)], hg_send)
    for j in range(8):
        out_copy(j).wait()


def hand_over(loss_ref, hg_in, tg_in, loss_out, hg_out, tg_out, held, in_sem, out_sem):
    def copies(j):
        spot = pl.ds(j * (tg_in.shape[0] // PIECES), tg_in.shape[0] // PIECES)
        return (
            pltpu.make_async_copy(tg_in.at[spot], held.at[spot], in_sem.at[j]),
            pltpu.make_async_copy(held.at[spot], tg_out.at[spot], out_sem.at[j]),
        )

    for j in range(PIECES):
        copies(j)[0].start()
    loss_out[...] = loss_ref[0:1, : loss_out.shape[1]]
    hg_out[...] = hg_in[...]
    for j in range(PIECES):
        copies(j)[0].wait()
        copies(j)[1].start()
    for j in range(PIECES):
        copies(j)[1].wait()


def on_device(hidden, table, targets, owners, rows, input_grad):
    nz = lax.axis_size("dp") // 2
    nv = lax.axis_size("vocab")
    tokens, width = hidden.shape
    vocab_part = table.shape[0]
    half = vocab_part // 2
    block = tokens // nz
    groups = block // 8
    half_ring = nz // 2
    f32, bf16 = jnp.float32, jnp.bfloat16
    vmem = pl.BlockSpec(memory_space=pltpu.VMEM)
    hbm = pl.BlockSpec(memory_space=pl.ANY)
    dma = pltpu.SemaphoreType.DMA
    loss, hidden_grad, table_grad = pl.pallas_call(
        functools.partial(head_kernel, nz, nv),
        out_shape=(
            jax.ShapeDtypeStruct((8, LANES), f32),
            jax.ShapeDtypeStruct((block, width), bf16),
            jax.ShapeDtypeStruct((vocab_part, width), f32),
        ),
        in_specs=[vmem, vmem, vmem, vmem, hbm, hbm],
        out_specs=(vmem, vmem, hbm),
        scratch_shapes=[
            pltpu.VMEM((tokens, 2 * width), bf16),
            pltpu.VMEM((half, 2 * width), bf16),
            pltpu.VMEM((vocab_part, width), bf16),
            pltpu.VMEM((nz, block, half), f32),
            pltpu.VMEM((2, half_ring, block, half), f32),
            pltpu.VMEM((2, nz, groups, 16, half // 2), bf16),
            pltpu.VMEM((tokens, vocab_part), bf16),
            pltpu.VMEM((vocab_part, width), f32),
            pltpu.VMEM((nz, block, width), f32),
            pltpu.VMEM((tokens, width), bf16),
            pltpu.VMEM((nz, block, LANES), jnp.int32),
            pltpu.VMEM((nz, block + PAD, width), bf16),
            pltpu.VMEM((nv, block + PAD, width), bf16),
            pltpu.VMEM((nv, block, width), f32),
            pltpu.VMEM((block, LANES), f32),
            pltpu.VMEM((2, 8, LANES), f32),
            pltpu.VMEM((nv, 8, LANES), f32),
            pltpu.VMEM((nz, 8, LANES), f32),
            dma((3,)),
            dma((1 + CHUNKS,)),
            dma((1 + CHUNKS,)),
            dma((2, 2)),
            dma((2, half_ring, groups)),
            dma((2, 2)),
            dma((2, half_ring, groups)),
            dma,
            dma((nz,)),
            *[dma] * 10,
            dma((8,)),
        ],
        compiler_params=pltpu.CompilerParams(
            collective_id=0, has_side_effects=True, vmem_limit_bytes=58 * 1024 * 1024
        ),
        name="head",
    )(
        targets, rows, owners.reshape(1, tokens),
        input_grad, hidden, table,
    )
    token_loss, hidden_grad, table_grad = pl.pallas_call(
        hand_over,
        out_shape=(
            jax.ShapeDtypeStruct((1, block // 2), f32),
            jax.ShapeDtypeStruct((block, width), bf16),
            jax.ShapeDtypeStruct((vocab_part, width), f32),
        ),
        in_specs=[vmem, vmem, hbm],
        out_specs=(vmem, vmem, hbm),
        scratch_shapes=[pltpu.VMEM((vocab_part, width), f32), dma((PIECES,)), dma((PIECES,))],
        compiler_params=pltpu.CompilerParams(vmem_limit_bytes=58 * 1024 * 1024),
        name="hand_over",
    )(loss, hidden_grad, table_grad)
    return (token_loss.reshape(block // 2), hidden_grad, table_grad)


def solution(mesh):
    return jax.shard_map(
        on_device,
        mesh=mesh,
        in_specs=(P(None, "dp"), P("vocab", "dp"), P(), P(), P(), P("vocab", "dp")),
        out_specs=(P("dp"), P("vocab", "dp"), P("vocab", "dp")),
        check_vma=False,
    )
```

time: 455 us -> 100 us (0.22)
  waiting for transfers between devices: 336 us -> 0 us
  Pallas kernels: 0 us -> 99.1 us
  blocking collectives: 62.1 us -> 0 us
  matrix products: 18.3 us -> 0 us
  between operations: 14.8 us -> 0.64 us
  other arithmetic: 12.9 us -> 0 us
  local copies, waits for them, and re-layouts: 6.5 us -> 0 us
    psum x1 -> x0, waiting for transfers between devices: 227 us -> none  [on_device(): lax.psum(lax.dot_general(picked, table, (((1,), (1,)), ((), ())), preferr...]
    unnamed x3 -> x0, waiting for transfers between devices: 103 us -> none
    pallas_call x0 -> x2, Pallas kernels: none -> 99.1 us  [the longest x1 95 us: on_device(): pl.pallas_call(functools.partial(head_kernel, nz, nv), out_shape=(jax.Sha...]
    pmax x1 -> x0, blocking collectives: 33.1 us -> none  [combine_stats(): largest = lax.pmax(local_max, 'vocab')]
    psum x1 -> x0, blocking collectives: 29 us -> none  [combine_stats(): totals = lax.psum((local_exp, local_target), 'vocab')]
    dot_general x5 -> x0, matrix products: 18.3 us -> none  [the longest x1 5.58 us: on_device(): lax.dot_general(slot_rows, incoming.reshape(slot_total, width_part), (((0...]
    all_to_all x1 -> x0, waiting for transfers between devices: 5.2 us -> none  [on_device(): lax.all_to_all(outgoing.reshape(vocab_count, capacity, width_part), 'voca...]
    convert_element_type x2 -> x0, other arithmetic: 4.78 us -> none  [the longest x1 3.33 us: on_device(): (jnp.exp(logits - log_total[:, None]) - aimed.astype(jnp.float32)).astype...]
  transfers between devices with their start and end apart: 3 -> 0, of which waited for: 3 -> 0; matrix products, arithmetic and copies ran while one was open for 3% -> 0% of each run, Pallas kernels for 0% -> 0%
where the time goes in v2:
time: 100 us; the launch traced here: 99.8 us
  Pallas kernels  99.1 us (99%)
    pallas_call x1, Pallas kernels, on_device(): pl.pallas_call(functools.partial(head_kernel, nz, nv), out_shape=(jax.Sha...  95 us
    pallas_call x1, Pallas kernels, on_device(): pl.pallas_call(hand_over, out_shape=(jax.ShapeDtypeStruct((1, block // 2)...  4.16 us

profile of v2, /device:TPU:1, one launch (start us, length us, event | category | flops | bytes accessed | tf_op | source)
XLA Modules:
  0.0 99.8 jit_solution(1720122409122328713)
XLA Ops:
  0.6 95.0 %head.1 = (f32[8,128]{1,0:T(8,128)}, bf16[40,384]{1,0:T(8,128)(2,1)}, f32[2048,384]{1,0:T(8,128)}) custom-call(s32[640]{0:T(1024)} %targets_ref.1, s32[640]{0:T(1024)} %rows_ref.1, s32[1,640]{1,0:T(1,128)} %bitcast.2, bf16[40,384]{1,0:T(8,128)(2,1)} %ig_ref.1, bf16[640,384]{1,0:T(8,128)(2,1)} %hidden_hbm.1, bf16[2048,384]{1,0:T(8,128)(2,1)} %table_hbm.1), custom_call_target="tpu_custom_call" | custom-call | tf_op jit(solution)/shard_map/head/pallas_call | solution.py:475
  95.6 4.2 %hand_over.1 = (f32[1,20]{1,0:T(1,128)}, bf16[40,384]{1,0:T(8,128)(2,1)}, f32[2048,384]{1,0:T(8,128)}) custom-call(f32[8,128]{1,0:T(8,128)} %get-tuple-element.9.loss_ref, bf16[40,384]{1,0:T(8,128)(2,1)} %get-tuple-element.10.hg_in, f32[2048,384]{1,0:T(8,128)} %get-tuple-element.11.tg_in), custom_call_target="tpu_custom_call" | custom-call | tf_op jit(solution)/shard_map/hand_over/pallas_call | solution.py:523

commit v3 on v2

--- a/solution.py
+++ b/solution.py
@@ -11,7 +11,6 @@
 MESH = pl.DeviceIdType.MESH
 LANES = 128
 CHUNKS = 4
-PAD = 8
 PIECES = 8
 AG_TREE = {7: 5}
 AG_ORDER = (1, 2, 3, 4, 5, 6, 7, 8)
@@ -25,7 +24,7 @@
     hgs, hgr, igs, mst, st1, st2, stz,
     load_sem, give_send, give_recv, rs_send, rs_recv, ag_send, ag_recv, core_send, core_recv,
     st1_send, st1_recv, st2_send, st2_recv, stz_send, stz_recv, ig_send, ig_recv,
-    hg_send, hg_recv, out_sem,
+    hg_send, hg_recv, cross_send, cross_recv, pass_send, pass_recv, out_sem,
 ):
     half_ring = nz // 2
     tree = {b: AG_TREE.get(b, b - 1) if nz == 16 else b - 1 for b in range(1, half_ring + 1)}
@@ -52,6 +51,7 @@
 
     near = {"dp": z * 2 + (1 - c)}
     step_to = tuple(zdev(sign) for sign in signs)
+    cross_to = tuple({"dp": at_z(sign) * 2 + (1 - c)} for sign in signs)
 
     def nearby(k):
         return at_z(jnp.where(k % 2 == 1, -((k + 1) // 2), k // 2))
@@ -74,15 +74,27 @@
     for copy in loads:
         copy.start()
 
-    @pl.loop(1, nz)
-    def _(i):
-        pl.semaphore_signal(barrier, inc=1, device_id=zdev(i), device_id_type=MESH)
+    spans = {signs[way] * (b - a) for way in range(2) for b, a in tree.items()}
+    heard = [
+        {-b for b in range(1, half_ring + 1)} | spans,
+        {b for b in range(1, half_ring)} | spans,
+    ]
+    heard = [sorted({offset % nz for offset in some}) for some in heard]
+    for core in range(2):
+        @pl.when(c == core)
+        def _(core=core):
+            for offset in heard[core]:
+                pl.semaphore_signal(barrier, inc=1, device_id=zdev(offset), device_id_type=MESH)
+
+    for device in cross_to:
+        pl.semaphore_signal(barrier, inc=1, device_id=device, device_id_type=MESH)
 
     @pl.loop(1, nv)
     def _(i):
         pl.semaphore_signal(barrier, inc=1, device_id={"vocab": peer(i)}, device_id_type=MESH)
 
-    pl.semaphore_wait(barrier, nz + nv - 1)
+    told = jnp.where(c == 0, len(heard[0]), len(heard[1]))
+    pl.semaphore_wait(barrier, told + 3 + nv - 1)
 
     chunk = half // CHUNKS
     gives = [remote(hidden_hbm, hidc.at[:, my_lanes], give_send.at[0], give_recv.at[0], near)]
@@ -203,8 +215,16 @@
     def st2_copy(i):
         return remote(st2.at[v], st2.at[v], st2_send, st2_recv, {"vocab": peer(i)})
 
-    def stz_copy(i):
-        return remote(stz.at[z], stz.at[z], stz_send, stz_recv, zdev(i))
+    below = stz.at[pl.ds(1, half_ring)]
+    above = stz.at[pl.ds(half_ring + 1, half_ring - 1)]
+
+    def stz_copy(b):
+        return remote(
+            stz.at[0], stz.at[c * half_ring + b], stz_send, stz_recv, zdev((1 - 2 * c) * b)
+        )
+
+    def slot_of(k):
+        return jnp.where(k % 2 == 1, (k + 1) // 2, jnp.where(k == 0, 0, half_ring + k // 2))
 
     def pack(a, b, c):
         return jnp.where(sub == 0, a, jnp.where(sub == 1, b, c))
@@ -221,10 +241,19 @@
             zdev(signs[way] * (b - a)),
         )
 
+    def cross_copy(way, g, side):
+        lanes = pl.ds(way * (quarter // 2), quarter // 2)
+        ref = g_all.at[side, at_z(-signs[way] * (half_ring - 1)), g, :, lanes]
+        if side is not c:
+            ref = g_all.at[side, at_z(half_ring), g, :, lanes]
+        return remote(ref, ref, cross_send, cross_recv.at[way, g], cross_to[way])
+
     def ag_on(way, a, g):
         for b in sorted(tree):
             if tree[b] == a:
                 ag_copy(way, b, g).start()
+                if b == half_ring:
+                    cross_copy(way, g, c).start()
 
     def core_copy(k, side):
         ref = g_all.at[side, nearby(k)]
@@ -237,8 +266,8 @@
                 ag_copy(way, b, g).wait_recv()
                 ag_on(way, b, g)
 
-        core_copy(2 * b - 1, c).start()
         if b < half_ring:
+            core_copy(2 * b - 1, c).start()
             core_copy(2 * b, c).start()
 
     def finish_logits():
@@ -291,15 +320,19 @@
         target = jnp.sum(t, axis=0, keepdims=True)
         mine = jnp.exp(st1[0, 0:1, :] - log_total)
         other = jnp.exp(st1[1, 0:1, :] - log_total)
-        stz[z] = pack(
+        stz[0] = pack(
             jnp.where(c == 0, mine, other),
             jnp.where(c == 0, other, mine),
             jnp.exp(target - log_total) - 1.0,
         )
 
-        @pl.loop(1, nz)
-        def _(i):
-            stz_copy(i).start()
+        @pl.loop(1, half_ring)
+        def _(b):
+            stz_copy(b).start()
+
+        @pl.when(c == 0)
+        def _():
+            stz_copy(half_ring).start()
 
         pick = lax.broadcasted_iota(jnp.int32, (block, LANES), 0) == (
             lax.broadcasted_iota(jnp.int32, (block, LANES), 1) + c * (block // 2)
@@ -309,20 +342,35 @@
             (8, LANES),
         )
 
+    def stz_pass():
+        for core, mine in ((0, below), (1, above)):
+            @pl.when(c == core)
+            def _(mine=mine):
+                remote(mine, mine, stz_send, stz_recv, near).wait_recv()
+                remote(mine, mine, pass_send, pass_recv, near).start()
+
     def stz_wait():
-        rest = stz.at[pl.ds(1, nz - 1)]
-        remote(rest, rest, stz_send, stz_recv, near).wait_recv()
+        for core, other in ((0, above), (1, below)):
+            @pl.when(c == core)
+            def _(other=other):
+                remote(other, other, pass_send, pass_recv, near).wait_recv()
 
     def core_wait(first, last):
-        for k in range(first, last):
+        for k in range(first, min(last, nz - 1)):
             core_copy(k, 1 - c).wait_recv()
+        if last == nz:
+            @pl.loop(0, groups)
+            def _(g):
+                for way in range(2):
+                    cross_copy(way, g, 1 - c).wait_recv()
 
     def gradients(first, last):
         @pl.loop(first // 2, last // 2)
         def _(j):
             rows = pl.ds(pl.multiple_of(j * 2 * block, 16), 2 * block)
             ds = [nearby(2 * j), nearby(2 * j + 1)]
-            factors = [[as_col(stz[d, r : r + 1, :]) for r in range(3)] for d in ds]
+            slots = [slot_of(2 * j), slot_of(2 * j + 1)]
+            factors = [[as_col(stz[i, r : r + 1, :]) for r in range(3)] for i in slots]
             wanted = [tcol[d, :, 0:1] - first_col for d in ds]
             for side in range(2):
                 for q in range(2):
@@ -350,8 +398,10 @@
         terms = jnp.dot(
             gn[first * block : last * block, :], tab[...], preferred_element_type=jnp.float32
         ).reshape(last - first, block, width)
-        low = jnp.concatenate([terms, jnp.zeros((last - first, PAD, width), jnp.float32)], axis=1)
-        hgs[first:last] = low.astype(jnp.bfloat16)
+        tiles = [terms[:, :, i : i + LANES] for i in range(0, width, LANES)]
+        rest = hgs.shape[1] - block * len(tiles)
+        tiles.append(jnp.zeros((last - first, rest, LANES), jnp.float32))
+        hgs[first:last] = jnp.concatenate(tiles, axis=1).astype(jnp.bfloat16)
 
         @pl.loop(first, last)
         def _(k):
@@ -366,8 +416,9 @@
 
         rest = hgr.at[pl.ds(1, nv - 1)]
         remote(rest, rest, hg_send, hg_recv, near).wait_recv()
-        hg_ref[...] = (
-            logit_scale * jnp.sum(hgr[...].astype(jnp.float32)[:, :block], axis=0)
+        total = logit_scale * jnp.sum(hgr[...].astype(jnp.float32), axis=0)
+        hg_ref[...] = jnp.concatenate(
+            [total[i * block : (i + 1) * block] for i in range(width // LANES)], axis=1
         ).astype(jnp.bfloat16)
 
     def head(j):
@@ -396,11 +447,17 @@
     stats_core()
     todo = {
         2: [stats_final],
-        5: [stz_wait, lambda: core_wait(0, nz // 2), lambda: gradients(0, nz // 2)],
+        5: [stz_pass],
+        6: [stz_wait, lambda: core_wait(0, nz // 4), lambda: gradients(0, nz // 4)],
         7: [
+            lambda: core_wait(nz // 4, nz // 2),
+            lambda: gradients(nz // 4, nz // 2),
             lambda: hidden_terms(0, nz // 2),
             lambda: core_wait(nz // 2, third),
             lambda: gradients(nz // 2, third),
+            lambda: hidden_terms(nz // 2, third),
+            lambda: core_wait(third, nz - 2),
+            lambda: gradients(third, nz - 2),
         ],
     }
     for b in AG_ORDER if nz == 16 else range(1, half_ring + 1):
@@ -410,9 +467,8 @@
     for b in sorted(todo):
         for act in todo[b]:
             act()
-    hidden_terms(nz // 2, third)
-    core_wait(third, nz)
-    gradients(third, nz)
+    core_wait(nz - 2, nz)
+    gradients(nz - 2, nz)
     hidden_terms(third, nz)
     for j in range(8):
         head(j)
@@ -431,10 +487,16 @@
         all_sent(ring.at[way, pl.ds(1, half_ring - 1)], rs_send.at[way, 1])
         all_sent(g_all.at[c, pl.ds(1, half_ring - 1)], ag_send.at[way, 0])
         all_sent(g_all.at[c, 0, :, :, pl.ds(0, quarter // 2)], ag_send.at[way, 1])
-    all_sent(g_all.at[c], core_send)
+    all_sent(g_all.at[c, pl.ds(1, nz - 1)], core_send)
+    all_sent(g_all.at[c, 0], cross_send)
     all_sent(igs.at[pl.ds(1, nv - 1)], ig_send)
     all_sent(st2.at[pl.ds(1, nv - 1)], st2_send)
-    all_sent(stz.at[pl.ds(1, nz - 1)], stz_send)
+    for core, mine in ((0, below), (1, above)):
+        @pl.when(c == core)
+        def _(mine=mine):
+            all_sent(mine, stz_send)
+            all_sent(mine, pass_send)
+
     all_sent(hgs.at[pl.ds(1, nv - 1)], hg_send)
     for j in range(8):
         out_copy(j).wait()
@@ -468,6 +530,7 @@
     block = tokens // nz
     groups = block // 8
     half_ring = nz // 2
+    packed = -(-block * (width // LANES) // 16) * 16
     f32, bf16 = jnp.float32, jnp.bfloat16
     vmem = pl.BlockSpec(memory_space=pltpu.VMEM)
     hbm = pl.BlockSpec(memory_space=pl.ANY)
@@ -493,8 +556,8 @@
             pltpu.VMEM((nz, block, width), f32),
             pltpu.VMEM((tokens, width), bf16),
             pltpu.VMEM((nz, block, LANES), jnp.int32),
-            pltpu.VMEM((nz, block + PAD, width), bf16),
-            pltpu.VMEM((nv, block + PAD, width), bf16),
+            pltpu.VMEM((nz, packed, LANES), bf16),
+            pltpu.VMEM((nv, packed, LANES), bf16),
             pltpu.VMEM((nv, block, width), f32),
             pltpu.VMEM((block, LANES), f32),
             pltpu.VMEM((2, 8, LANES), f32),
@@ -510,6 +573,10 @@
             dma,
             dma((nz,)),
             *[dma] * 10,
+            dma,
+            dma((2, groups)),
+            dma,
+            dma,
             dma((8,)),
         ],
         compiler_params=pltpu.CompilerParams(

time: 100 us -> 96.9 us (0.969)
  the two profiles are of different devices: /device:TPU:1 before, /device:TPU:16 now
where the time goes in v3:
time: 96.9 us; the launch traced here: 96.6 us
  Pallas kernels  96 us (99%)
    pallas_call x1, Pallas kernels, on_device(): pl.pallas_call(functools.partial(head_kernel, nz, nv), out_shape=(jax.Sha...  91.8 us
    pallas_call x1, Pallas kernels, on_device(): pl.pallas_call(hand_over, out_shape=(jax.ShapeDtypeStruct((1, block // 2)...  4.16 us

profile of v3, /device:TPU:16, one launch (start us, length us, event | category | flops | bytes accessed | tf_op | source)
XLA Modules:
  0.0 96.6 jit_solution(5261334280336428730)
XLA Ops:
  0.6 91.8 %head.1 = (f32[8,128]{1,0:T(8,128)}, bf16[40,384]{1,0:T(8,128)(2,1)}, f32[2048,384]{1,0:T(8,128)}) custom-call(s32[640]{0:T(1024)} %targets_ref.1, s32[640]{0:T(1024)} %rows_ref.1, s32[1,640]{1,0:T(1,128)} %bitcast.2, bf16[40,384]{1,0:T(8,128)(2,1)} %ig_ref.1, bf16[640,384]{1,0:T(8,128)(2,1)} %hidden_hbm.1, bf16[2048,384]{1,0:T(8,128)(2,1)} %table_hbm.1), custom_call_target="tpu_custom_call" | custom-call | tf_op jit(solution)/shard_map/head/pallas_call | solution.py:538
  92.4 4.2 %hand_over.1 = (f32[1,20]{1,0:T(1,128)}, bf16[40,384]{1,0:T(8,128)(2,1)}, f32[2048,384]{1,0:T(8,128)}) custom-call(f32[8,128]{1,0:T(8,128)} %get-tuple-element.9.loss_ref, bf16[40,384]{1,0:T(8,128)(2,1)} %get-tuple-element.10.hg_in, f32[2048,384]{1,0:T(8,128)} %get-tuple-element.11.tg_in), custom_call_target="tpu_custom_call" | custom-call | tf_op jit(solution)/shard_map/hand_over/pallas_call | solution.py:590

commit v4 on v3

--- a/solution.py
+++ b/solution.py
@@ -18,9 +18,9 @@
 
 def head_kernel(
     nz, nv,
-    targets_ref, rows_ref, owners_ref, ig_ref, hidden_hbm, table_hbm,
+    targets_hbm, rows_hbm, owners_hbm, ig_ref, hidden_hbm, table_hbm,
     loss_ref, hg_ref, tg_hbm,
-    hidc, tabc, tab, part, ring, g_all, gn, acc, hid32, hid_near, tcol,
+    targets_ref, rows_ref, owners_ref, hidc, tabc, tab, part, ring, g_all, gn, acc, hid32, hid_near, tcol,
     hgs, hgr, igs, mst, st1, st2, stz,
     load_sem, give_send, give_recv, rs_send, rs_recv, ag_send, ag_recv, core_send, core_recv,
     st1_send, st1_recv, st2_send, st2_recv, stz_send, stz_recv, ig_send, ig_recv,
@@ -68,11 +68,12 @@
         pltpu.make_async_copy(hidden_hbm, hidc.at[:, my_lanes], load_sem.at[0]),
         pltpu.make_async_copy(table_hbm.at[my_half], tabc.at[:, my_lanes], load_sem.at[1]),
         pltpu.make_async_copy(table_hbm, tab, load_sem.at[2]),
+        pltpu.make_async_copy(targets_hbm, targets_ref, load_sem.at[3]),
+        pltpu.make_async_copy(rows_hbm, rows_ref, load_sem.at[4]),
+        pltpu.make_async_copy(owners_hbm, owners_ref, load_sem.at[5]),
     ]
     barrier = pltpu.get_barrier_semaphore()
     pl.semaphore_signal(barrier, inc=1, device_id=near, device_id_type=MESH)
-    for copy in loads:
-        copy.start()
 
     spans = {signs[way] * (b - a) for way in range(2) for b, a in tree.items()}
     heard = [
@@ -93,6 +94,8 @@
     def _(i):
         pl.semaphore_signal(barrier, inc=1, device_id={"vocab": peer(i)}, device_id_type=MESH)
 
+    for copy in loads:
+        copy.start()
     told = jnp.where(c == 0, len(heard[0]), len(heard[1]))
     pl.semaphore_wait(barrier, told + 3 + nv - 1)
 
@@ -153,6 +156,8 @@
             rs_open(0)
     rs_open(1)
 
+    for copy in loads[3:]:
+        copy.wait()
     igs[v] = ig_ref[...].astype(jnp.float32)
 
     def ig_copy(i):
@@ -419,7 +424,7 @@
         total = logit_scale * jnp.sum(hgr[...].astype(jnp.float32), axis=0)
         hg_ref[...] = jnp.concatenate(
             [total[i * block : (i + 1) * block] for i in range(width // LANES)], axis=1
-        ).astype(jnp.bfloat16)
+        )
 
     def head(j):
         spot = (pl.ds(j * piece, piece), slice(None))
@@ -446,7 +451,7 @@
     third = 3 * nz // 8 * 2
     stats_core()
     todo = {
-        2: [stats_final],
+        3: [stats_final],
         5: [stz_pass],
         6: [stz_wait, lambda: core_wait(0, nz // 4), lambda: gradients(0, nz // 4)],
         7: [
@@ -502,7 +507,9 @@
         out_copy(j).wait()
 
 
-def hand_over(loss_ref, hg_in, tg_in, loss_out, hg_out, tg_out, held, in_sem, out_sem):
+def hand_over(
+    loss_in, hg_in, tg_in, loss_out, hg_out, tg_out, loss_ref, hg_ref, held, small_sem, in_sem, out_sem
+):
     def copies(j):
         spot = pl.ds(j * (tg_in.shape[0] // PIECES), tg_in.shape[0] // PIECES)
         return (
@@ -510,13 +517,21 @@
             pltpu.make_async_copy(held.at[spot], tg_out.at[spot], out_sem.at[j]),
         )
 
+    small = [
+        pltpu.make_async_copy(loss_in, loss_ref, small_sem.at[0]),
+        pltpu.make_async_copy(hg_in, hg_ref, small_sem.at[1]),
+    ]
+    for copy in small:
+        copy.start()
     for j in range(PIECES):
         copies(j)[0].start()
-    loss_out[...] = loss_ref[0:1, : loss_out.shape[1]]
-    hg_out[...] = hg_in[...]
     for j in range(PIECES):
         copies(j)[0].wait()
         copies(j)[1].start()
+    for copy in small:
+        copy.wait()
+    loss_out[...] = loss_ref[0:1, : loss_out.shape[1]]
+    hg_out[...] = hg_ref[...].astype(jnp.bfloat16)
     for j in range(PIECES):
         copies(j)[1].wait()
 
@@ -539,12 +554,15 @@
         functools.partial(head_kernel, nz, nv),
         out_shape=(
             jax.ShapeDtypeStruct((8, LANES), f32),
-            jax.ShapeDtypeStruct((block, width), bf16),
+            jax.ShapeDtypeStruct((block, width), f32),
             jax.ShapeDtypeStruct((vocab_part, width), f32),
         ),
-        in_specs=[vmem, vmem, vmem, vmem, hbm, hbm],
+        in_specs=[hbm, hbm, hbm, vmem, hbm, hbm],
         out_specs=(vmem, vmem, hbm),
         scratch_shapes=[
+            pltpu.VMEM((tokens,), jnp.int32),
+            pltpu.VMEM((tokens,), jnp.int32),
+            pltpu.VMEM((1, tokens), jnp.int32),
             pltpu.VMEM((tokens, 2 * width), bf16),
             pltpu.VMEM((half, 2 * width), bf16),
             pltpu.VMEM((vocab_part, width), bf16),
@@ -563,7 +581,7 @@
             pltpu.VMEM((2, 8, LANES), f32),
             pltpu.VMEM((nv, 8, LANES), f32),
             pltpu.VMEM((nz, 8, LANES), f32),
-            dma((3,)),
+            dma((6,)),
             dma((1 + CHUNKS,)),
             dma((1 + CHUNKS,)),
             dma((2, 2)),
@@ -594,9 +612,16 @@
             jax.ShapeDtypeStruct((block, width), bf16),
             jax.ShapeDtypeStruct((vocab_part, width), f32),
         ),
-        in_specs=[vmem, vmem, hbm],
+        in_specs=[hbm] * 3,
         out_specs=(vmem, vmem, hbm),
-        scratch_shapes=[pltpu.VMEM((vocab_part, width), f32), dma((PIECES,)), dma((PIECES,))],
+        scratch_shapes=[
+            pltpu.VMEM((8, LANES), f32),
+            pltpu.VMEM((block, width), f32),
+            pltpu.VMEM((vocab_part, width), f32),
+            dma((2,)),
+            dma((PIECES,)),
+            dma((PIECES,)),
+        ],
         compiler_params=pltpu.CompilerParams(vmem_limit_bytes=58 * 1024 * 1024),
         name="hand_over",
     )(loss, hidden_grad, table_grad)

time: 96.9 us -> 95.3 us (0.983)
  the two profiles are of different devices: /device:TPU:16 before, /device:TPU:1 now
where the time goes in v4:
time: 95.3 us; the launch traced here: 93.9 us
  Pallas kernels  93.3 us (98%)
    pallas_call x1, Pallas kernels, on_device(): pl.pallas_call(functools.partial(head_kernel, nz, nv), out_shape=(jax.Sha...  89.8 us
    pallas_call x1, Pallas kernels, on_device(): pl.pallas_call(hand_over, out_shape=(jax.ShapeDtypeStruct((1, block // 2)...  3.42 us

profile of v4, /device:TPU:1, one launch (start us, length us, event | category | flops | bytes accessed | tf_op | source)
XLA Modules:
  0.0 93.9 jit_solution(15420587133095638715)
XLA Ops:
  0.6 89.8 %head.1 = (f32[8,128]{1,0:T(8,128)}, f32[40,384]{1,0:T(8,128)}, f32[2048,384]{1,0:T(8,128)}) custom-call(s32[640]{0:T(1024)} %targets_hbm.1, s32[640]{0:T(1024)} %rows_hbm.1, s32[1,640]{1,0:T(1,128)} %bitcast.2, bf16[40,384]{1,0:T(8,128)(2,1)} %ig_ref.1, bf16[640,384]{1,0:T(8,128)(2,1)} %hidden_hbm.1, bf16[2048,384]{1,0:T(8,128)(2,1)} %table_hbm.1), custom_call_target="tpu_custom_call" | custom-call | tf_op jit(solution)/shard_map/head/pallas_call | solution.py:553
  90.5 3.4 %hand_over.1 = (f32[1,20]{1,0:T(1,128)}, bf16[40,384]{1,0:T(8,128)(2,1)}, f32[2048,384]{1,0:T(8,128)}) custom-call(f32[8,128]{1,0:T(8,128)} %get-tuple-element.9.loss_in, f32[40,384]{1,0:T(8,128)} %get-tuple-element.10.hg_in, f32[2048,384]{1,0:T(8,128)} %get-tuple-element.11.tg_in), custom_call_target="tpu_custom_call" | custom-call | tf_op jit(solution)/shard_map/hand_over/pallas_call | solution.py:608
